TPU v7x, 1024 devices: a whole 8x8x8 slice. The times are simulated.
1024 devices in a mesh: row: 16 (over z_hi, x), col: 64 (over z_lo, y, core).
Axes of the slice: x: 8, y: 8, z: 8 (z_hi: 2, z_lo: 4; z = z_hi * 4 + z_lo), core: 2. Of those that a mesh axis runs over, the one named last changes fastest.
Arguments:
- integrals: float32 [9600, 76800], P('row', 'col'), may hold values from -0.0234375 to 0.0234375
- amplitudes: float32 [512, 64, 1200], P('col', None, 'row'), may hold values from -16 to 16
- old_amps: float32 [512, 9600], P('col', 'row'), may hold values from -2 to 2
- other_terms: float32 [512, 9600], P('col', 'row'), may hold values from -6 to 6
- occ_energy: float32 [128], replicated, may hold values from -2 to -0.5
- vir_energy: float32 [1200], replicated, may hold values from 0.2 to 4
- pair_occ: int32 [512, 2], P('col'), may hold values from 0 to 127
- a_orbitals: int32 [8], replicated, may hold values from 0 to 1199
Outputs:
- new_amps: float32 [512, 9600], P('col', 'row')
All inputs are finite; a program needn't handle non-finite values.
Results may differ from a plain program's by a relative error of at most 0.00005.
Values sent between devices are 32-bit elements; how exact they have to be, the bound alone decides.
A program may use at most 32 MiB of HBM per device.

v0:
```python
import jax
import jax.numpy as jnp
from jax import lax
from jax.sharding import PartitionSpec as P

NV = 1200


def local(
    integrals, amplitudes, old_amps, other_terms, occ_energy, vir_energy, pair_occ, a_orbitals
):
    rows_here = integrals.shape[0]
    panel = lax.all_to_all(amplitudes, "col", split_axis=1, concat_axis=0, tiled=True)
    partial_value = lax.dot_general(
        lax.all_gather(panel, "row", axis=2, tiled=True)[:, 0, :],
        integrals,
        (((1,), (1,)), ((), ())),
        precision=lax.Precision.HIGHEST,
        preferred_element_type=jnp.float32,
    )
    ladder = lax.psum_scatter(partial_value, "col", scatter_dimension=0, tiled=True)
    occ_table = jnp.arange(occ_energy.shape[0], dtype=jnp.int32)
    occ_first = jnp.sum(
        jnp.where(pair_occ[:, 0:1] == occ_table[None, :], occ_energy[None, :], 0.0), axis=1
    )
    occ_second = jnp.sum(
        jnp.where(pair_occ[:, 1:2] == occ_table[None, :], occ_energy[None, :], 0.0), axis=1
    )
    first_row = lax.axis_index("row") * rows_here
    a_local = first_row // NV
    b_offset = first_row % NV
    a_pick = lax.dynamic_slice_in_dim(a_orbitals, a_local, 1, 0)
    vir_table = jnp.arange(NV, dtype=jnp.int32)
    vir_a = jnp.sum(jnp.where(vir_table == a_pick[0], vir_energy, 0.0))
    vir_b = lax.dynamic_slice_in_dim(vir_energy, b_offset, rows_here, 0)
    denom = (occ_first + occ_second)[:, None] - (vir_a + vir_b)[None, :]
    return old_amps + (ladder + other_terms) / denom


def solution(mesh):
    in_specs = (
        P("row", "col"),
        P("col", None, "row"),
        P("col", "row"),
        P("col", "row"),
        P(),
        P(),
        P("col", None),
        P(),
    )
    out_specs = P("col", "row")
    return jax.shard_map(local, mesh=mesh, in_specs=in_specs, out_specs=out_specs, check_vma=False)
```

profile of v0, /device:TPU:1, one launch (start us, length us, event | category | flops | bytes accessed | tf_op | source)
XLA Modules:
  0.0 707.5 jit_solution(3730731224603490248)
XLA Ops:
  6.5 0.0 copy-start
  6.5 0.0 all-gather.2.cloned.1.call-start
  6.5 1.3 copy.13
  7.8 29.9 %all_to_all.18 = f32[8,64,75]{2,0,1:T(8,128)S(1)} all-to-all(f32[8,64,75]{2,0,1:T(8,128)S(1)} %copy.13), channel_id=1, replica_groups=mesh['row'=16,'col'=64] {'col'}, dimensions={1} | all-to-all | bytes 307200 | tf_op jit(solution)/shard_map/all_to_all | solution.py:13
  37.6 0.8 copy.14
  38.4 0.0 all-gather.2.cloned.1.call-update
  38.5 0.0 copy-start.6
  38.5 0.0 copy-start.4
  38.5 0.0 copy-start.5
  38.5 0.0 copy-start.3
  38.5 0.0 copy-start.1
  38.5 0.0 copy-start.2
  38.5 0.0 all-reduce.3.cloned.1.call-start
  38.6 116.1 %all-gather.2.cloned.1.call-done = f32[512,1,1200]{0,1,2:T(1,128)} async-done(((f32[512,1,75]{0,1,2:T(1,128)}), f32[512,1,1200]{0,1,2:T(1,128)}) %all-gather.2.cloned.1.call-update) | async-done | bytes 2457616 | tf_op jit(solution)/shard_map/all_gather | solution.py:15
  154.7 0.0 copy-done
  154.7 15.2 %fusion = f32[512,600]{1,0:T(8,128)} fusion(f32[600,1200]{1,0:T(8,128)S(1)} %copy-done, f32[512,1,1200]{0,1,2:T(1,128)} %all-gather.2.cloned.1.call-done), kind=kOutput, calls=%fused_computation | convolution fusion | flops 4423680000 | bytes 6566400 | tf_op jit(solution)/shard_map/dot_general | solution.py:14
  169.9 0.0 all-reduce.3.cloned.1.call-update
  170.0 1.3 dynamic-slice
  171.9 0.0 copy-done.6
  171.9 0.6 dynamic_slice.6
  172.5 0.0 copy-done.4
  172.5 0.0 copy-done.5
  172.5 0.2 select_reduce_fusion.1
  172.7 0.0 copy-done.3
  172.7 1.3 select_reduce_fusion
  174.0 0.7 dynamic-slice_add_fusion.1
  174.7 524.6 %all-reduce.3.cloned.1.call-done = f32[512,600]{1,0:T(8,128)} async-done(((f32[512,600]{1,0:T(8,128)}), f32[512,600]{1,0:T(8,128)}) %all-reduce.3.cloned.1.call-update) | async-done | bytes 1228816
  699.3 0.0 copy-done.1
  699.3 0.0 copy-done.2
  699.3 1.4 fusion.4
  (2 shorter events, 0.0 us)
Async XLA Ops:
  6.5 148.2 %copy-start = (f32[600,1200]{1,0:T(8,128)S(1)}, f32[600,1200]{1,0:T(8,128)}, u32[]{:S(2)}) copy-start(f32[600,1200]{1,0:T(8,128)} %param.8) | copy-start | bytes 8640004
  6.5 148.2 %all-gather.2.cloned.1.call-start = ((), (), s32[]{:S(2)}) async-start(), calls=%async_computation.1 | async-start | bytes 2611200 | tf_op jit(solution)/shard_map/all_gather | solution.py:15
  38.5 133.4 %copy-start.6 = (s32[8]{0:T(128)S(1)}, s32[8]{0:T(128)}, u32[]{:S(2)}) copy-start(s32[8]{0:T(128)} %param.15) | copy-start | bytes 100
  38.5 134.0 %copy-start.4 = (s32[8,2]{0,1:T(2,128)S(1)}, s32[8,2]{0,1:T(2,128)}, u32[]{:S(2)}) copy-start(s32[8,2]{0,1:T(2,128)} %param.14) | copy-start | bytes 196
  38.5 134.0 %copy-start.5 = (f32[128]{0:T(128)S(1)}, f32[128]{0:T(128)}, u32[]{:S(2)}) copy-start(f32[128]{0:T(128)} %param.12) | copy-start | bytes 1540
  38.5 134.2 %copy-start.3 = (f32[1200]{0:T(1024)S(1)}, f32[1200]{0:T(1024)}, u32[]{:S(2)}) copy-start(f32[1200]{0:T(1024)} %param.13) | copy-start | bytes 14404
  38.5 660.8 %copy-start.1 = (f32[8,600]{1,0:T(8,128)S(1)}, f32[8,600]{1,0:T(8,128)}, u32[]{:S(2)}) copy-start(f32[8,600]{1,0:T(8,128)} %param.10) | copy-start | bytes 57604
  38.5 660.8 %copy-start.2 = (f32[8,600]{1,0:T(8,128)S(1)}, f32[8,600]{1,0:T(8,128)}, u32[]{:S(2)}) copy-start(f32[8,600]{1,0:T(8,128)} %param.11) | copy-start | bytes 57604
  38.5 660.7 %all-reduce.3.cloned.1.call-start = ((), (), s32[]{:S(2)}) async-start(), calls=%async_computation.2 | async-start | bytes 2621440
Sparse Core Ops, SparseCore 0:
  38.6 116.0 all-gather.1
  170.0 529.2 all-reduce.2
where the time goes:
time: 708 us
  waiting for transfers between devices  641 us (91%)
  blocking collectives  29.9 us (4%)
  matrix products  15.2 us (2%)
  between operations  14.2 us (2%)
    unnamed x3, waiting for transfers between devices  525 us
    all_gather x1, waiting for transfers between devices, local(): lax.all_gather(panel, 'row', axis=2, tiled=True)[:, 0, :]  116 us
    all_to_all x1, blocking collectives, local(): lax.all_to_all(amplitudes, 'col', split_axis=1, concat_axis=0, tiled=True)  29.9 us
    dot_general x1, matrix products, local(): lax.dot_general(lax.all_gather(panel, 'row', axis=2, tiled=True)[:, 0, :]...  15.2 us
  transfers between devices with their start and end apart: 2, of which 2 were waited for; matrix products, arithmetic and copies ran while one was open for 1% of the time, Pallas kernels for 0%

commit v1 on v0

v1 whole, which is shorter than its diff:
```python
import jax
import jax.numpy as jnp
from jax import lax
from jax.experimental import pallas as pl
from jax.experimental.pallas import tpu as pltpu
from jax.sharding import PartitionSpec as P

NV = 1200
MESH = pl.DeviceIdType.MESH
X = 8
PLANE = 16
STAGES = 4
ROWS = 16
DEPTH = 75
UNIT = 80
AB = 600
ABP = 640
F32 = jnp.float32
BF16 = jnp.bfloat16

RIGHT_OWN, RIGHT_OTHER, LEFT_OWN, LEFT_OTHER = 0, 4, 7, 10


def kernel(
    integrals_ref,
    amps_ref,
    old_ref,
    other_ref,
    occ_ref,
    vir_ref,
    pair_ref,
    aorb_ref,
    out_ref,
    integ,
    staged,
    relay,
    tiles,
    units,
    factors,
    total,
    partial,
    from_core,
    from_y,
    to_z,
    from_z,
    integ_sem,
    bundle_send,
    bundle_recv,
    tile_send,
    tile_recv,
    unit_send,
    unit_recv,
    core_send,
    core_recv,
    y_send,
    y_recv,
    z_send,
    z_recv,
):
    r = lax.axis_index("row")
    k = lax.axis_index("col")
    x, zh = r % X, r // X
    zl, m = k // PLANE, k % PLANE
    y, core = m // 2, m % 2
    right = zh * X + (x + 1) % X
    left = zh * X + (x + X - 1) % X
    facing = (r + X) % ROWS

    load = pltpu.make_async_copy(integrals_ref, integ, integ_sem)
    load.start()

    barrier = pltpu.get_barrier_semaphore()

    def greet(row, col):
        pl.semaphore_signal(barrier, inc=1, device_id=(row, col), device_id_type=MESH)

    def greet_plane(j, carry):
        greet(r, zl * PLANE + (m + j) % PLANE)
        return carry

    lax.fori_loop(1, PLANE, greet_plane, 0)
    for j in range(1, STAGES):
        greet(r, ((zl + j) % STAGES) * PLANE + m)
    greet(right, k)
    greet(left, k)
    greet(facing, k)

    def stage_tiles(o, carry):
        for j in range(8):
            c = o * 8 + j
            staged[c] = jnp.zeros((8, 128), F32)
            staged[c, :, 0:DEPTH] = amps_ref[pl.ds(c, 8, stride=64), :]
        return carry

    lax.fori_loop(0, 8, stage_tiles, 0)
    pl.semaphore_wait(barrier, PLANE - 1 + STAGES - 1 + 3)

    def send_tiles(i, source, base):
        def one(j, carry):
            t = (m + j) % PLANE
            pltpu.make_async_remote_copy(
                src_ref=source.at[base + t],
                dst_ref=tiles.at[i, m],
                send_sem=tile_send.at[i],
                recv_sem=tile_recv.at[i],
                device_id=(r, zl * PLANE + t),
                device_id_type=MESH,
            ).start()
            return carry

        lax.fori_loop(1, PLANE, one, 0)
        tiles[i, m] = source[base + m]

    def bundle(i):
        plane = (zl + STAGES - i) % STAGES
        return pltpu.make_async_remote_copy(
            src_ref=staged.at[pl.ds(plane * PLANE, PLANE)],
            dst_ref=relay.at[pl.ds(i * PLANE, PLANE)],
            send_sem=bundle_send.at[i],
            recv_sem=bundle_recv.at[i],
            device_id=(r, plane * PLANE + m),
            device_id_type=MESH,
        )

    send_tiles(0, staged, zl * PLANE)
    for i in range(1, STAGES):
        bundle(i).start()

    load.wait()

    def make_factors(d, rows, count):
        lane = lax.broadcasted_iota(jnp.int32, (count, 128), 1)
        first, off = (DEPTH * d) // 128 * 128, (DEPTH * d) % 128

        def tile_at(start):
            width = min(128, NV - start)
            v = integ[rows, start : start + width]
            if width < 128:
                v = jnp.concatenate([v, jnp.zeros((count, 128 - width), F32)], axis=1)
            return v

        v = tile_at(first)
        if off:
            v = pltpu.roll(v, 128 - off, 1)
        if off + DEPTH > 128:
            v = jnp.where(lane < 128 - off, v, pltpu.roll(tile_at(first + 128), 128 - off, 1))
        v = jnp.where(lane < DEPTH, v, 0.0)
        hi = v.astype(BF16).astype(F32)
        lo = pltpu.roll(v - hi, UNIT, 1)
        return (
            (hi + jnp.where(lane >= UNIT, lo, 0.0)).astype(BF16),
            (pltpu.roll(hi, 2 * UNIT - 128, 1) + jnp.where(lane < 32, lo, 0.0)).astype(BF16),
        )

    for d in range(ROWS):

        def chunk(n, carry, d=d):
            rows = pl.ds(pl.multiple_of(n * 128, 128), 128)
            a, b = make_factors(d, rows, 128)
            factors[d, rows, 0:128] = a
            factors[d, rows, 128:256] = b
            return carry

        lax.fori_loop(0, 4, chunk, 0)
        a, b = make_factors(d, slice(512, AB), AB - 512)
        pad = jnp.zeros((ABP - AB, 128), BF16)
        factors[d, 512:ABP, 0:128] = jnp.concatenate([a, pad], axis=0)
        factors[d, 512:ABP, 128:256] = jnp.concatenate([b, pad], axis=0)

    def hop(i, lane, h):
        to_right = lane in (RIGHT_OWN, RIGHT_OTHER)
        own = lane in (RIGHT_OWN, LEFT_OWN)
        at = (x + X - (h - 1)) % X if to_right else (x + h - 1) % X
        origin = (zh if own else 1 - zh) * X + at
        return pltpu.make_async_remote_copy(
            src_ref=units.at[i, origin],
            dst_ref=units.at[i, origin],
            send_sem=unit_send.at[i],
            recv_sem=unit_recv.at[i, lane + h],
            device_id=(right if to_right else left, k),
            device_id_type=MESH,
        )

    def land(i, lane, h):
        to_right = lane in (RIGHT_OWN, RIGHT_OTHER)
        own = lane in (RIGHT_OWN, LEFT_OWN)
        at = (x + X - h) % X if to_right else (x + h) % X
        origin = (zh if own else 1 - zh) * X + at
        pltpu.make_async_remote_copy(
            src_ref=units.at[i, origin],
            dst_ref=units.at[i, origin],
            send_sem=unit_send.at[i],
            recv_sem=unit_recv.at[i, lane + h],
            device_id=(right, k),
            device_id_type=MESH,
        ).wait_recv()
        return origin

    def across(i, origin):
        return pltpu.make_async_remote_copy(
            src_ref=units.at[i, origin],
            dst_ref=units.at[i, origin],
            send_sem=unit_send.at[i],
            recv_sem=unit_recv.at[i, 0],
            device_id=(facing, k),
            device_id_type=MESH,
        )

    def add(i, origin, first=False):
        a = units[i, origin]
        hi = a.astype(BF16)
        lo = (a - hi.astype(F32)).astype(BF16)
        rhs = jnp.concatenate([hi, hi, lo, jnp.zeros((256 - 3 * UNIT, 128), BF16)], axis=0)
        product = jnp.dot(factors[origin], rhs, preferred_element_type=F32)
        if first:
            total[i] = product
        else:
            total[i] += product

    def begin(i):
        pltpu.make_async_copy(
            tiles.at[i, pl.ds(0, PLANE - 1)], tiles.at[i, pl.ds(0, PLANE - 1)], tile_recv.at[i]
        ).wait()
        units[i, r] = jnp.transpose(tiles[i].reshape(128, 128))[0:UNIT]
        across(i, r).start()
        hop(i, RIGHT_OWN, 1).start()
        hop(i, LEFT_OWN, 1).start()

    def pass_on(i):
        bundle(i).wait_recv()
        send_tiles(i, relay, i * PLANE)

    def step(i, s):
        got = []
        if s == 1:
            across(i, facing).wait_recv()
            hop(i, RIGHT_OTHER, 1).start()
            hop(i, LEFT_OTHER, 1).start()
            got.append(facing)
        for lane, hops, h in (
            (RIGHT_OWN, 4, s),
            (LEFT_OWN, 3, s),
            (RIGHT_OTHER, 3, s - 1),
            (LEFT_OTHER, 4, s - 1),
        ):
            if 1 <= h <= hops:
                got.append(land(i, lane, h))
                if h < hops:
                    hop(i, lane, h + 1).start()
        return got

    def core_copy(i):
        return pltpu.make_async_remote_copy(
            src_ref=partial.at[i, 1 - core],
            dst_ref=from_core.at[i],
            send_sem=core_send.at[i],
            recv_sem=core_recv.at[i],
            device_id=(r, zl * PLANE + y * 2 + 1 - core),
            device_id_type=MESH,
        )

    def sum_cores(i):
        ladder = jnp.transpose(total[i])
        for t in range(PLANE):
            partial[i, t % 2, t // 2] = ladder[8 * t : 8 * t + 8]
        core_copy(i).start()

    def sum_y(i):
        core_copy(i).wait_recv()
        partial[i, core] = partial[i, core] + from_core[i]

        def one(j, carry):
            t = (y + j) % 8
            pltpu.make_async_remote_copy(
                src_ref=partial.at[i, core, t],
                dst_ref=from_y.at[i, y],
                send_sem=y_send.at[i],
                recv_sem=y_recv.at[i],
                device_id=(r, zl * PLANE + t * 2 + core),
                device_id_type=MESH,
            ).start()
            return carry

        lax.fori_loop(1, 8, one, 0)
        from_y[i, y] = partial[i, core, y]

    def z_copy(i):
        return pltpu.make_async_remote_copy(
            src_ref=to_z.at[i],
            dst_ref=from_z.at[i],
            send_sem=z_send.at[i],
            recv_sem=z_recv.at[i],
            device_id=(r, ((zl + i) % STAGES) * PLANE + m),
            device_id_type=MESH,
        )

    def sum_z(i):
        seven = from_y.at[i, pl.ds(0, 7)]
        pltpu.make_async_copy(seven, seven, y_recv.at[i]).wait()
        value = from_y[i, 0]
        for j in range(1, 8):
            value = value + from_y[i, j]
        to_z[i] = value

    def drain(i):
        some = units.at[i, pl.ds(0, 15)]
        pltpu.make_async_copy(some, some, unit_send.at[i]).wait()
        some = tiles.at[i, pl.ds(0, PLANE - 1)]
        pltpu.make_async_copy(some, some, tile_send.at[i]).wait()
        core_copy(i).wait_send()
        some = from_y.at[i, pl.ds(0, 7)]
        pltpu.make_async_copy(some, some, y_send.at[i]).wait()

    def turn(n, carry):
        @pl.when(n < STAGES)
        def _():
            begin(n)

        @pl.when((n >= 1) & (n < STAGES + 1))
        def _():
            origins = step(n - 1, 2)
            for origin in origins:
                add(n - 1, origin)

        @pl.when(n >= 2)
        def _():
            origins = step(n - 2, 4)
            for origin in origins:
                add(n - 2, origin)

        @pl.when(n < STAGES)
        def _():
            add(n, r, first=True)

        @pl.when(n < STAGES - 1)
        def _():
            pass_on(n + 1)

        @pl.when(n >= 3)
        def _():
            sum_y(n - 3)

        @pl.when(n < STAGES)
        def _():
            origins = step(n, 1)
            for origin in origins:
                add(n, origin)

        @pl.when((n >= 1) & (n < STAGES + 1))
        def _():
            origins = step(n - 1, 3)
            for origin in origins:
                add(n - 1, origin)

        @pl.when(n >= 2)
        def _():
            origins = step(n - 2, 5)
            for origin in origins:
                add(n - 2, origin)
            sum_cores(n - 2)

        @pl.when(n >= 3)
        def _():
            sum_z(n - 3)

        @pl.when(n >= 4)
        def _():
            z_copy(n - 3).start()

        @pl.when(n >= 3)
        def _():
            drain(n - 3)

        return carry

    lax.fori_loop(0, STAGES + 2, turn, 0)

    last = STAGES - 1
    sum_y(last)

    pair = pair_ref[...]
    table = lax.broadcasted_iota(jnp.int32, (8, 128), 1)
    occ = occ_ref[...]
    occ_first = jnp.sum(jnp.where(pair[:, 0:1] == table, occ, 0.0), axis=1, keepdims=True)
    occ_second = jnp.sum(jnp.where(pair[:, 1:2] == table, occ, 0.0), axis=1, keepdims=True)
    vir = vir_ref[...]
    blocks = lax.broadcasted_iota(jnp.int32, (1, 8), 1)
    a_pick = jnp.sum(
        jnp.where(blocks == r // 2, aorb_ref[...].astype(F32), 0.0), axis=1, keepdims=True
    )
    orbitals = lax.broadcasted_iota(jnp.int32, (1, NV), 1).astype(F32)
    vir_a = jnp.sum(jnp.where(orbitals == a_pick, vir, 0.0), axis=1, keepdims=True)
    vir_b = jnp.where(r % 2 == 0, vir[:, 0:AB], vir[:, AB:NV])
    denom = (occ_first + occ_second) - (vir_a + vir_b)

    sum_z(last)
    z_copy(last).start()
    for i in range(1, STAGES):
        bundle(i).wait_send()
    drain(last)
    ladder = to_z[0]
    for i in range(1, STAGES):
        z_copy(i).wait_recv()
        ladder = ladder + from_z[i]
    out_ref[...] = old_ref[...] + (ladder[:, 0:AB] + other_ref[...]) / denom
    for i in range(1, STAGES):
        z_copy(i).wait_send()


def local(
    integrals, amplitudes, old_amps, other_terms, occ_energy, vir_energy, pair_occ, a_orbitals
):
    vmem = pl.BlockSpec(memory_space=pltpu.VMEM)
    dma = pltpu.SemaphoreType.DMA
    return pl.pallas_call(
        kernel,
        out_shape=jax.ShapeDtypeStruct((8, AB), F32),
        in_specs=[pl.BlockSpec(memory_space=pl.ANY)] + [vmem] * 7,
        out_specs=vmem,
        scratch_shapes=[
            pltpu.VMEM((AB, NV), F32),
            pltpu.VMEM((64, 8, 128), F32),
            pltpu.VMEM((64, 8, 128), F32),
            pltpu.VMEM((STAGES, PLANE, 8, 128), F32),
            pltpu.VMEM((STAGES, ROWS, UNIT, 128), F32),
            pltpu.VMEM((ROWS, ABP, 256), BF16),
            pltpu.VMEM((STAGES, ABP, 128), F32),
            pltpu.VMEM((STAGES, 2, 8, 8, ABP), F32),
            pltpu.VMEM((STAGES, 8, 8, ABP), F32),
            pltpu.VMEM((STAGES, 8, 8, ABP), F32),
            pltpu.VMEM((STAGES, 8, ABP), F32),
            pltpu.VMEM((STAGES, 8, ABP), F32),
            dma,
            dma((STAGES,)),
            dma((STAGES,)),
            dma((STAGES,)),
            dma((STAGES,)),
            dma((STAGES,)),
            dma((STAGES, 15)),
            dma((STAGES,)),
            dma((STAGES,)),
            dma((STAGES,)),
            dma((STAGES,)),
            dma((STAGES,)),
            dma((STAGES,)),
        ],
        compiler_params=pltpu.CompilerParams(
            collective_id=0, has_side_effects=True, vmem_limit_bytes=40 * 1024 * 1024
        ),
        cost_estimate=pl.CostEstimate(
            flops=6 * 512 * AB * NV, bytes_accessed=4 * AB * NV, transcendentals=0
        ),
    )(
        integrals,
        amplitudes.reshape(8 * 64, DEPTH),
        old_amps,
        other_terms,
        occ_energy.reshape(1, -1),
        vir_energy.reshape(1, -1),
        pair_occ,
        a_orbitals.reshape(1, -1),
    )


def solution(mesh):
    in_specs = (
        P("row", "col"),
        P("col", None, "row"),
        P("col", "row"),
        P("col", "row"),
        P(),
        P(),
        P("col", None),
        P(),
    )
    out_specs = P("col", "row")
    return jax.shard_map(local, mesh=mesh, in_specs=in_specs, out_specs=out_specs, check_vma=False)
```

time: 708 us -> 99.6 us (0.14)
  the two profiles are of different devices: /device:TPU:1 before, /device:TPU:4 now
where the time goes in v1:
time: 99.6 us; the launch traced here: 99.2 us
  Pallas kernels  91.6 us (92%)
  local copies, waits for them, and re-layouts  7.64 us (8%)
    pallas_call x1, Pallas kernels, local(): pl.pallas_call(kernel, out_shape=jax.ShapeDtypeStruct((8, AB), F32), in_s...  91.6 us
    unnamed x14, local copies, waits for them, and re-layouts  6.94 us

profile of v1, /device:TPU:4, one launch (start us, length us, event | category | flops | bytes accessed | tf_op | source)
XLA Modules:
  0.0 99.2 jit_solution(16556415905005807972)
XLA Ops:
  0.0 0.8 copy.9.pair_ref
  0.8 0.7 reshape.14.vir_ref
  1.5 0.0 copy-start
  1.5 1.9 %copy-done = f32[600,1200]{1,0:T(8,128)S(1)} copy-done((f32[600,1200]{1,0:T(8,128)S(1)}, f32[600,1200]{1,0:T(8,128)}, u32[]{:S(2)}) %copy-start) | copy-done | bytes 2880024
  3.3 0.0 copy-start.1
  3.3 0.9 copy-done.1
  4.3 0.0 copy-start.2
  4.3 0.7 copy-done.2
  5.0 0.0 copy-start.3
  5.0 0.7 copy-done.3
  5.7 0.0 copy-start.4
  5.7 0.7 copy-done.4
  6.4 0.0 copy-start.5
  6.4 0.7 copy-done.5
  7.0 91.6 %shard_map.82 = f32[8,600]{1,0:T(8,128)S(1)} custom-call(f32[600,1200]{1,0:T(8,128)S(1)} %copy-done, f32[512,75]{1,0:T(8,128)S(1)} %bitcast.3, f32[8,600]{1,0:T(8,128)S(1)} %copy-done.2, f32[8,600]{1,0:T(8,128)S(1)} %copy-done.3, f32[1,128]{1,0:T(1,128)S(1)} %bitcast.4, f32[1,1200]{1,0:T(1,128)S(1)} %reshape.14.vir_ref, s32[8,2]{1,0:T(8,128)S(1)} %copy.9.pair_ref, ...), custom_call_target="tpu_custom_call" | custom-call | flops 2211840000 | bytes 2880000 | tf_op jit(solution)/shard_map/pallas_call | solution.py:415
  98.6 0.6 copy.11
Async XLA Ops:
  1.5 1.9 %copy-start = (f32[600,1200]{1,0:T(8,128)S(1)}, f32[600,1200]{1,0:T(8,128)}, u32[]{:S(2)}) copy-start(f32[600,1200]{1,0:T(8,128)} %integrals_ref.1) | copy-start | bytes 8640004
  3.3 0.9 copy-start.1
  4.3 0.7 copy-start.2
  5.0 0.7 copy-start.3
  5.7 0.7 copy-start.4
  6.4 0.7 copy-start.5

commit v2 on v1

v2 whole, which is shorter than its diff:
```python
import jax
import jax.numpy as jnp
from jax import lax
from jax.experimental import pallas as pl
from jax.experimental.pallas import tpu as pltpu
from jax.sharding import PartitionSpec as P

NV = 1200
MESH = pl.DeviceIdType.MESH
X = 8
PLANE = 16
STAGES = 4
ROWS = 16
DEPTH = 75
UNIT = 80
AB = 600
ABP = 640
NVP = 1280
WINDOW = 768
SHIFT = 88
F32 = jnp.float32
BF16 = jnp.bfloat16

RIGHT_OWN, RIGHT_OTHER, LEFT_OWN, LEFT_OTHER = 0, 4, 7, 10


def far_first(n, count):
    return count // 2 + (n + 1) // 2 * (1 - 2 * (n % 2))


def kernel(
    integrals_hbm,
    amps_hbm,
    old_hbm,
    other_hbm,
    occ_hbm,
    vir_hbm,
    pair_hbm,
    aorb_hbm,
    out_ref,
    integ,
    amps_ref,
    old_ref,
    other_ref,
    occ_ref,
    vir_ref,
    pair_ref,
    aorb_ref,
    staged,
    relay,
    tiles,
    units,
    high,
    low,
    panel,
    total,
    partial,
    from_core,
    from_y,
    to_z,
    from_z,
    facing_here,
    load_sem,
    bundle_send,
    bundle_recv,
    tile_send,
    tile_recv,
    unit_send,
    unit_recv,
    core_send,
    core_recv,
    y_send,
    y_recv,
    z_send,
    z_recv,
):
    r = lax.axis_index("row")
    k = lax.axis_index("col")
    x, zh = r % X, r // X
    zl, m = k // PLANE, k % PLANE
    y, core = m // 2, m % 2
    right = zh * X + (x + 1) % X
    left = zh * X + (x + X - 1) % X
    facing = (r + X) % ROWS

    loads = [
        pltpu.make_async_copy(source, target, load_sem.at[n])
        for n, (source, target) in enumerate(
            (
                (amps_hbm, amps_ref),
                (integrals_hbm, integ),
                (old_hbm, old_ref),
                (other_hbm, other_ref),
                (occ_hbm, occ_ref),
                (vir_hbm, vir_ref),
                (pair_hbm, pair_ref),
                (aorb_hbm, aorb_ref),
            )
        )
    ]
    loads[0].start()

    barrier = pltpu.get_barrier_semaphore()

    def greet(row, col):
        pl.semaphore_signal(barrier, inc=1, device_id=(row, col), device_id_type=MESH)

    def greet_plane(j, carry):
        greet(r, zl * PLANE + (m + j) % PLANE)
        return carry

    lax.fori_loop(1, PLANE, greet_plane, 0)
    for j in range(1, STAGES):
        greet(r, ((zl + j) % STAGES) * PLANE + m)
    greet(right, k)
    greet(left, k)

    @pl.when(zh == 0)
    def _():
        greet(facing, k)


    def stage_tiles(o, carry):
        for j in range(8):
            c = o * 8 + j
            staged[c] = jnp.zeros((8, 128), F32)
            staged[c, :, 0:DEPTH] = amps_ref[pl.ds(c, 8, stride=64), :]
        return carry

    loads[0].wait()
    for load in loads[1:]:
        load.start()
    lax.fori_loop(0, 8, stage_tiles, 0)
    pl.semaphore_wait(barrier, PLANE - 1 + STAGES - 1 + 2 + zh)

    @pl.when(zh == 1)
    def _():
        pl.semaphore_signal(facing_here, inc=1, device_id=(facing, k), device_id_type=MESH)


    def send_tiles(i, source, base):
        def one(n, carry):
            t = (m + far_first(n, PLANE)) % PLANE
            pltpu.make_async_remote_copy(
                src_ref=source.at[base + t],
                dst_ref=tiles.at[i, m],
                send_sem=tile_send.at[i],
                recv_sem=tile_recv.at[i],
                device_id=(r, zl * PLANE + t),
                device_id_type=MESH,
            ).start()
            return carry

        lax.fori_loop(0, PLANE - 1, one, 0)
        tiles[i, m] = source[base + m]

    def bundle(i):
        plane = (zl + STAGES - i) % STAGES
        return pltpu.make_async_remote_copy(
            src_ref=staged.at[pl.ds(plane * PLANE, PLANE)],
            dst_ref=relay.at[pl.ds(i * PLANE, PLANE)],
            send_sem=bundle_send.at[i],
            recv_sem=bundle_recv.at[i],
            device_id=(r, plane * PLANE + m),
            device_id_type=MESH,
        )

    send_tiles(0, staged, zl * PLANE)
    for i in range(1, STAGES):
        bundle(i).start()

    def split(v):
        hi = v.astype(BF16)
        return hi, (v - hi.astype(F32)).astype(BF16)

    def split_integrals():
        loads[1].wait()
        last = NV // 128 * 128
        for part in (high, low):
            part[:, last:] = jnp.zeros((ABP, NVP - last), BF16)

        def chunk(n, carry):
            rows = pl.ds(pl.multiple_of(n * 128, 128), 128)
            hi, lo = split(integ[rows, :])
            high[rows, 0:NV] = hi
            low[rows, 0:NV] = lo
            return carry

        lax.fori_loop(0, 4, chunk, 0)
        pad = jnp.zeros((ABP - AB, NV), BF16)
        hi, lo = split(integ[512:AB, :])
        high[512:ABP, 0:NV] = jnp.concatenate([hi, pad], axis=0)
        low[512:ABP, 0:NV] = jnp.concatenate([lo, pad], axis=0)

    def hop(i, lane, h):
        to_right = lane in (RIGHT_OWN, RIGHT_OTHER)
        own = lane in (RIGHT_OWN, LEFT_OWN)
        at = (x + X - (h - 1)) % X if to_right else (x + h - 1) % X
        origin = (zh if own else 1 - zh) * X + at
        return pltpu.make_async_remote_copy(
            src_ref=units.at[i, origin],
            dst_ref=units.at[i, origin],
            send_sem=unit_send.at[i],
            recv_sem=unit_recv.at[i, lane + h],
            device_id=(right if to_right else left, k),
            device_id_type=MESH,
        )

    def land(i, lane, h):
        to_right = lane in (RIGHT_OWN, RIGHT_OTHER)
        own = lane in (RIGHT_OWN, LEFT_OWN)
        at = (x + X - h) % X if to_right else (x + h) % X
        origin = (zh if own else 1 - zh) * X + at
        pltpu.make_async_remote_copy(
            src_ref=units.at[i, origin],
            dst_ref=units.at[i, origin],
            send_sem=unit_send.at[i],
            recv_sem=unit_recv.at[i, lane + h],
            device_id=(right, k),
            device_id_type=MESH,
        ).wait_recv()
        return origin

    def across(i, origin):
        return pltpu.make_async_remote_copy(
            src_ref=units.at[i, origin],
            dst_ref=units.at[i, origin],
            send_sem=unit_send.at[i],
            recv_sem=unit_recv.at[i, 0],
            device_id=(facing, k),
            device_id_type=MESH,
        )

    def add(i, plane):
        for u in range(X):
            panel[plane, pl.ds(plane * SHIFT + u * DEPTH, DEPTH), :] = units[
                i, plane * X + u, 0:DEPTH
            ]
        columns = pl.ds(pl.multiple_of(plane * 512, 128), WINDOW)
        hi, lo = split(panel[plane])
        both = jnp.dot(
            high[:, columns], jnp.concatenate([hi, lo], axis=1), preferred_element_type=F32
        )
        rest = jnp.dot(low[:, columns], hi, preferred_element_type=F32)
        total[i] += both[:, 0:128] + (both[:, 128:256] + rest)

    def produce(i):
        some = tiles.at[i, pl.ds(0, PLANE - 1)]
        pltpu.make_async_copy(some, some, tile_recv.at[i]).wait()
        units[i, r] = jnp.transpose(tiles[i].reshape(128, 128))[0:UNIT]

        @pl.when(zh == 1)
        def _():
            across(i, r).start()

    def pass_on(i):
        bundle(i).wait_recv()
        send_tiles(i, relay, i * PLANE)

    def step(i, s, own):
        rights, lefts = (RIGHT_OWN, LEFT_OWN) if own else (RIGHT_OTHER, LEFT_OTHER)
        if s == 0:
            if not own:
                across(i, facing).wait_recv()
            hop(i, rights, 1).start()
            hop(i, lefts, 1).start()
            return [r if own else facing]
        got = []
        for lane, hops in ((rights, 4 if own else 3), (lefts, 3 if own else 4)):
            if s <= hops:
                got.append(land(i, lane, s))
                if s < hops:
                    hop(i, lane, s + 1).start()
        return got

    def core_copy(i):
        return pltpu.make_async_remote_copy(
            src_ref=partial.at[i, 1 - core],
            dst_ref=from_core.at[i],
            send_sem=core_send.at[i],
            recv_sem=core_recv.at[i],
            device_id=(r, zl * PLANE + y * 2 + 1 - core),
            device_id_type=MESH,
        )

    def sum_cores(i):
        ladder = jnp.transpose(total[i])
        for t in range(PLANE):
            partial[i, t % 2, t // 2] = ladder[8 * t : 8 * t + 8]
        core_copy(i).start()

    def sum_y(i):
        core_copy(i).wait_recv()
        partial[i, core] = partial[i, core] + from_core[i]

        def one(n, carry):
            t = (y + far_first(n, 8)) % 8
            pltpu.make_async_remote_copy(
                src_ref=partial.at[i, core, t],
                dst_ref=from_y.at[i, y],
                send_sem=y_send.at[i],
                recv_sem=y_recv.at[i],
                device_id=(r, zl * PLANE + t * 2 + core),
                device_id_type=MESH,
            ).start()
            return carry

        lax.fori_loop(0, 7, one, 0)
        from_y[i, y] = partial[i, core, y]

    def z_copy(i):
        return pltpu.make_async_remote_copy(
            src_ref=to_z.at[i],
            dst_ref=from_z.at[i],
            send_sem=z_send.at[i],
            recv_sem=z_recv.at[i],
            device_id=(r, ((zl + i) % STAGES) * PLANE + m),
            device_id_type=MESH,
        )

    def sum_z(i):
        seven = from_y.at[i, pl.ds(0, 7)]
        pltpu.make_async_copy(seven, seven, y_recv.at[i]).wait()
        value = from_y[i, 0]
        for j in range(1, 8):
            value = value + from_y[i, j]
        to_z[i] = value

    def drain(i):
        some = units.at[i, pl.ds(0, 15)]
        pltpu.make_async_copy(some, some, unit_send.at[i]).wait()
        some = tiles.at[i, pl.ds(0, PLANE - 1)]
        pltpu.make_async_copy(some, some, tile_send.at[i]).wait()
        core_copy(i).wait_send()
        some = from_y.at[i, pl.ds(0, 7)]
        pltpu.make_async_copy(some, some, y_send.at[i]).wait()

    def within(n):
        return (n >= 0) & (n < STAGES)

    def own_step(n, s):
        @pl.when((n - s >= 0) & (n - s < 2))
        def _():
            for b in range(2):
                step((n - s) * 2 + b, s, True)

    total[...] = jnp.zeros_like(total)
    panel[...] = jnp.zeros_like(panel)
    split_integrals()
    pass_on(1)
    produce(0)
    step(0, 0, True)
    pass_on(2)
    pass_on(3)
    produce(1)
    step(1, 0, True)
    produce(2)
    produce(3)

    def turn(n, carry):
        for s in (4, 3, 2, 1):
            own_step(n, s)

        @pl.when(n == 1)
        def _():
            step(2, 0, True)
            step(3, 0, True)

        for s in (4, 3, 2, 1, 0):

            @pl.when(within(n - 3 - s))
            def _(s=s):
                step(n - 3 - s, s, False)

        @pl.when((n == 2) & (zh == 0))
        def _():
            pl.semaphore_wait(facing_here, 1)
            for i in range(STAGES):
                across(i, r).start()

        @pl.when(n >= 8)
        def _():
            sum_y(n - 8)

        @pl.when(within(n - 4))
        def _():
            add(n - 4, zh)

        @pl.when(within(n - 7))
        def _():
            add(n - 7, 1 - zh)
            sum_cores(n - 7)

        @pl.when(n == 10)
        def _():
            sum_z(0)

        return carry

    lax.fori_loop(1, 11, turn, 0)

    last = STAGES - 1
    sum_y(last)
    for i in (1, 2):
        sum_z(i)
        z_copy(i).start()

    for load in loads[2:]:
        load.wait()
    pair = jnp.transpose(
        jnp.concatenate(
            [
                jnp.concatenate([pair_ref[...].astype(F32), jnp.zeros((2, 120), F32)], axis=1),
                jnp.zeros((126, 128), F32),
            ],
            axis=0,
        )
    )[0:8]
    table = lax.broadcasted_iota(jnp.int32, (8, 128), 1).astype(F32)
    occ = occ_ref[...].reshape(1, 128)
    occ_first = jnp.sum(jnp.where(pair[:, 0:1] == table, occ, 0.0), axis=1, keepdims=True)
    occ_second = jnp.sum(jnp.where(pair[:, 1:2] == table, occ, 0.0), axis=1, keepdims=True)
    vir = vir_ref[...].reshape(1, NV)
    blocks = lax.broadcasted_iota(jnp.int32, (1, 8), 1)
    a_pick = jnp.sum(
        jnp.where(blocks == r // 2, aorb_ref[...].astype(F32).reshape(1, 8), 0.0),
        axis=1,
        keepdims=True,
    )
    orbitals = lax.broadcasted_iota(jnp.int32, (1, NV), 1).astype(F32)
    vir_a = jnp.sum(jnp.where(orbitals == a_pick, vir, 0.0), axis=1, keepdims=True)
    vir_b = jnp.where(r % 2 == 0, vir[:, 0:AB], vir[:, AB:NV])
    denom = (occ_first + occ_second) - (vir_a + vir_b)

    for i in range(1, STAGES):
        bundle(i).wait_send()
    for i in range(STAGES):
        drain(i)
    sum_z(last)
    z_copy(last).start()
    ladder = to_z[0]
    for i in range(1, STAGES):
        z_copy(i).wait_recv()
        ladder = ladder + from_z[i]
    out_ref[...] = old_ref[...] + (ladder[:, 0:AB] + other_ref[...]) / denom
    for i in range(1, STAGES):
        z_copy(i).wait_send()


def local(
    integrals, amplitudes, old_amps, other_terms, occ_energy, vir_energy, pair_occ, a_orbitals
):
    vmem = pl.BlockSpec(memory_space=pltpu.VMEM)
    dma = pltpu.SemaphoreType.DMA
    return pl.pallas_call(
        kernel,
        out_shape=jax.ShapeDtypeStruct((8, AB), F32),
        in_specs=[pl.BlockSpec(memory_space=pltpu.HBM)] * 8,
        out_specs=vmem,
        scratch_shapes=[
            pltpu.VMEM((AB, NV), F32),
            pltpu.VMEM((8 * 64, DEPTH), F32),
            pltpu.VMEM((8, AB), F32),
            pltpu.VMEM((8, AB), F32),
            pltpu.VMEM((128,), F32),
            pltpu.VMEM((NV,), F32),
            pltpu.VMEM((2, 8), jnp.int32),
            pltpu.VMEM((8,), jnp.int32),
            pltpu.VMEM((64, 8, 128), F32),
            pltpu.VMEM((64, 8, 128), F32),
            pltpu.VMEM((STAGES, PLANE, 8, 128), F32),
            pltpu.VMEM((STAGES, ROWS, UNIT, 128), F32),
            pltpu.VMEM((ABP, NVP), BF16),
            pltpu.VMEM((ABP, NVP), BF16),
            pltpu.VMEM((2, WINDOW, 128), F32),
            pltpu.VMEM((STAGES, ABP, 128), F32),
            pltpu.VMEM((STAGES, 2, 8, 8, ABP), F32),
            pltpu.VMEM((STAGES, 8, 8, ABP), F32),
            pltpu.VMEM((STAGES, 8, 8, ABP), F32),
            pltpu.VMEM((STAGES, 8, ABP), F32),
            pltpu.VMEM((STAGES, 8, ABP), F32),
            pltpu.SemaphoreType.REGULAR,
            dma((8,)),
            dma((STAGES,)),
            dma((STAGES,)),
            dma((STAGES,)),
            dma((STAGES,)),
            dma((STAGES,)),
            dma((STAGES, 15)),
            dma((STAGES,)),
            dma((STAGES,)),
            dma((STAGES,)),
            dma((STAGES,)),
            dma((STAGES,)),
            dma((STAGES,)),
        ],
        compiler_params=pltpu.CompilerParams(
            collective_id=0, has_side_effects=True, vmem_limit_bytes=60 * 1024 * 1024
        ),
        cost_estimate=pl.CostEstimate(
            flops=6 * 512 * AB * NV, bytes_accessed=4 * AB * NV, transcendentals=0
        ),
    )(
        integrals,
        amplitudes.reshape(8 * 64, DEPTH),
        old_amps,
        other_terms,
        occ_energy,
        vir_energy,
        pair_occ.T,
        a_orbitals,
    )


def solution(mesh):
    in_specs = (
        P("row", "col"),
        P("col", None, "row"),
        P("col", "row"),
        P("col", "row"),
        P(),
        P(),
        P("col", None),
        P(),
    )
    out_specs = P("col", "row")
    return jax.shard_map(local, mesh=mesh, in_specs=in_specs, out_specs=out_specs, check_vma=False)
```

time: 99.6 us -> 79.2 us (0.80)
  the two profiles are of different devices: /device:TPU:4 before, /device:TPU:1 now
where the time goes in v2:
time: 79.2 us; the launch traced here: 78.5 us
  Pallas kernels  77.1 us (97%)
  local copies, waits for them, and re-layouts  1.34 us (2%)
    pallas_call x1, Pallas kernels, local(): pl.pallas_call(kernel, out_shape=jax.ShapeDtypeStruct((8, AB), F32), in_s...  77.1 us

profile of v2, /device:TPU:1, one launch (start us, length us, event | category | flops | bytes accessed | tf_op | source)
XLA Modules:
  0.0 78.5 jit_solution(16784715845111132091)
XLA Ops:
  0.0 77.1 %shard_map.82 = f32[8,600]{1,0:T(8,128)} custom-call(f32[600,1200]{1,0:T(8,128)} %integrals_hbm.1, f32[512,75]{1,0:T(8,128)} %bitcast.2, f32[8,600]{1,0:T(8,128)} %old_hbm.1, f32[8,600]{1,0:T(8,128)} %other_hbm.1, f32[128]{0:T(128)} %occ_hbm.1, f32[1200]{0:T(1024)} %vir_hbm.1, s32[2,8]{1,0:T(2,128)} %bitcast.3, s32[8]{0:T(128)} %aorb_hbm.1), custom_call_target="tpu_custom_call" | custom-call | flops 2211840000 | bytes 2880000 | tf_op jit(solution)/shard_map/pallas_call | solution.py:455
  77.1 1.3 %copy.10 = f32[8,600]{1,0:T(8,128)} copy(f32[8,600]{1,0:T(8,128)} %shard_map.82) | data formatting | bytes 38400

commit v3 on v2

v3 whole, which is shorter than its diff:
```python
import jax
import jax.numpy as jnp
from jax import lax
from jax.experimental import pallas as pl
from jax.experimental.pallas import tpu as pltpu
from jax.sharding import PartitionSpec as P

NV = 1200
MESH = pl.DeviceIdType.MESH
X = 8
PLANE = 16
STAGES = 4
ROWS = 16
OTHER_TURN = 2
DEPTH = 75
UNIT = 80
AB = 600
ABP = 640
NVP = 1280
WINDOW = 768
SHIFT = 88
F32 = jnp.float32
BF16 = jnp.bfloat16

OWN_LONG, OWN_SHORT, OTHER_LONG, OTHER_SHORT = 0, 4, 7, 11


def far_first(n, count):
    return count // 2 + (n + 1) // 2 * (1 - 2 * (n % 2))


def kernel(
    integrals_hbm,
    amps_hbm,
    old_hbm,
    other_hbm,
    occ_hbm,
    vir_hbm,
    pair_hbm,
    aorb_hbm,
    out_ref,
    integ,
    amps_ref,
    old_ref,
    other_ref,
    occ_ref,
    vir_ref,
    pair_ref,
    aorb_ref,
    near_out,
    near_in,
    far_out,
    far_in,
    units_out,
    units,
    high,
    low,
    panel,
    total,
    partial,
    from_core,
    join,
    from_y,
    to_z,
    from_z,
    half_here,
    facing_here,
    load_sem,
    near_send,
    near_recv,
    far_send,
    far_recv,
    up_send,
    up_recv,
    unit_send,
    unit_recv,
    core_send,
    core_recv,
    join_recv,
    y_send,
    y_recv,
    z_send,
    z_recv,
):
    r = lax.axis_index("row")
    k = lax.axis_index("col")
    x, zh = r % X, r // X
    zl, m = k // PLANE, k % PLANE
    y, core = m // 2, m % 2
    right = zh * X + (x + 1) % X
    left = zh * X + (x + X - 1) % X
    facing = (r + X) % ROWS

    loads = [
        pltpu.make_async_copy(source, target, load_sem.at[n])
        for n, (source, target) in enumerate(
            (
                (amps_hbm, amps_ref),
                (integrals_hbm, integ),
                (old_hbm, old_ref),
                (other_hbm, other_ref),
                (occ_hbm, occ_ref),
                (vir_hbm, vir_ref),
                (pair_hbm, pair_ref),
                (aorb_hbm, aorb_ref),
            )
        )
    ]
    loads[0].start()

    barrier = pltpu.get_barrier_semaphore()

    def greet(row, col):
        pl.semaphore_signal(barrier, inc=1, device_id=(row, col), device_id_type=MESH)

    def greet_plane(j, carry):
        greet(r, zl * PLANE + (m + j) % PLANE)
        return carry

    lax.fori_loop(1, PLANE, greet_plane, 0)
    greet(right, k)
    greet(left, k)

    for j in range(1, STAGES):

        @pl.when(zl + j < STAGES)
        def _(j=j):
            greet(r, k + j * PLANE)

    @pl.when(zh == 0)
    def _():
        for j in range(STAGES):
            greet(facing, j * PLANE + m)

    def tile_of(plane, t):
        return amps_ref[pl.ds(plane % STAGES * PLANE + t, 8, stride=64), :]

    near_out[...] = jnp.zeros_like(near_out)
    far_out[...] = jnp.zeros_like(far_out)
    loads[0].wait()
    for load in loads[1:]:
        load.start()
    for t in range(PLANE):
        near_out[t, :, 0:DEPTH] = tile_of(zl, t)
    pl.semaphore_wait(barrier, PLANE - 1 + 2 + zl + STAGES * zh)

    def answer(sem, row, col):
        pl.semaphore_signal(sem, inc=1, device_id=(row, col), device_id_type=MESH)

    for j in range(1, STAGES):

        @pl.when(zl >= j)
        def _(j=j):
            answer(half_here, r, k - j * PLANE)

    @pl.when(zh == 1)
    def _():
        for j in range(STAGES):
            answer(facing_here, facing, j * PLANE + m)

    def send_tiles(source, target, send_sem, recv_sem):
        def one(n, carry):
            t = (m + far_first(n, PLANE)) % PLANE
            pltpu.make_async_remote_copy(
                src_ref=source.at[t],
                dst_ref=target.at[m],
                send_sem=send_sem,
                recv_sem=recv_sem,
                device_id=(r, zl * PLANE + t),
                device_id_type=MESH,
            ).start()
            return carry

        lax.fori_loop(0, PLANE - 1, one, 0)
        target[m] = source[m]

    def wait_for(some, sem):
        pltpu.make_async_copy(some, some, sem).wait()

    send_tiles(near_out, near_in, near_send, near_recv)
    for t in range(PLANE):
        for q in range(STAGES - 1):
            far_out[t, :, q * DEPTH : (q + 1) * DEPTH] = tile_of(zl + 1 + q, t)
    send_tiles(far_out, far_in, far_send, far_recv)

    def split(v):
        hi = v.astype(BF16)
        return hi, (v - hi.astype(F32)).astype(BF16)

    def split_integrals():
        loads[1].wait()
        last = NV // 128 * 128
        for part in (high, low):
            part[:, last:] = jnp.zeros((ABP, NVP - last), BF16)

        def chunk(n, carry):
            rows = pl.ds(pl.multiple_of(n * 128, 128), 128)
            hi, lo = split(integ[rows, :])
            high[rows, 0:NV] = hi
            low[rows, 0:NV] = lo
            return carry

        lax.fori_loop(0, 4, chunk, 0)
        pad = jnp.zeros((ABP - AB, NV), BF16)
        hi, lo = split(integ[512:AB, :])
        high[512:ABP, 0:NV] = jnp.concatenate([hi, pad], axis=0)
        low[512:ABP, 0:NV] = jnp.concatenate([lo, pad], axis=0)

    def way(i, lane):
        sign = 1 if lane in (OWN_LONG, OTHER_SHORT) else -1
        return sign * (1 - 2 * (i % 2))

    def copy_unit(i, lane, h, origin):
        return pltpu.make_async_remote_copy(
            src_ref=units.at[i, origin],
            dst_ref=units.at[i, origin],
            send_sem=unit_send.at[i],
            recv_sem=unit_recv.at[i, lane + h],
            device_id=(zh * X + (x + X + way(i, lane)) % X, k),
            device_id_type=MESH,
        )

    def origin_of(i, lane, h):
        plane = zh if lane in (OWN_LONG, OWN_SHORT) else 1 - zh
        return plane * X + (x + X - h * way(i, lane)) % X

    def hop(i, lane, h):
        return copy_unit(i, lane, h, origin_of(i, lane, h - 1))

    def land(i, lane, h):
        copy_unit(i, lane, h, origin_of(i, lane, h)).wait_recv()

    def add(i, plane):
        for u in range(X):
            panel[plane, pl.ds(plane * SHIFT + u * DEPTH, DEPTH), :] = units[
                i, plane * X + u, 0:DEPTH
            ]
        columns = pl.ds(pl.multiple_of(plane * 512, 128), WINDOW)
        hi, lo = split(panel[plane])
        both = jnp.dot(
            high[:, columns], jnp.concatenate([hi, lo], axis=1), preferred_element_type=F32
        )
        rest = jnp.dot(low[:, columns], hi, preferred_element_type=F32)
        total[i] += both[:, 0:128] + (both[:, 128:256] + rest)

    def unit_to(source, plane, row, recv_sem):
        return pltpu.make_async_remote_copy(
            src_ref=source,
            dst_ref=units.at[zl, r],
            send_sem=up_send,
            recv_sem=recv_sem,
            device_id=(row, plane * PLANE + m),
            device_id_type=MESH,
        )

    def to_half():
        for q in range(STAGES - 1):
            unit_to(units_out.at[q], (zl + 1 + q) % STAGES, r, up_recv.at[zl]).start()

    def to_facing():
        arrived = unit_recv.at[zl, 0]
        unit_to(units.at[zl, r], zl, facing, arrived).start()
        for q in range(STAGES - 1):
            unit_to(units_out.at[q], (zl + 1 + q) % STAGES, facing, arrived).start()

    def begin(i):
        @pl.when(zl != i)
        def _():
            wait_for(units.at[i, r], up_recv.at[i])

        step(i, 0, True)

    def make_units():
        wait_for(near_in.at[pl.ds(0, PLANE - 1)], near_recv)
        units[zl, r] = jnp.transpose(near_in[...].reshape(128, 128))[0:UNIT]
        wait_for(far_in.at[pl.ds(0, PLANE - 1)], far_recv)
        turned = jnp.transpose(far_in[...].reshape(128, 256))
        for q in range(STAGES - 1):
            units_out[q] = turned[q * DEPTH : q * DEPTH + UNIT]

    def step(i, s, own):
        long, short = (OWN_LONG, OWN_SHORT) if own else (OTHER_LONG, OTHER_SHORT)
        if s == 0 and not own:
            wait_for(units.at[i, facing], unit_recv.at[i, 0])
        for lane, hops in ((long, 4), (short, 3)):
            if 1 <= s <= hops:
                land(i, lane, s)
            if s < hops:
                hop(i, lane, s + 1).start()

    def core_copy(i):
        return pltpu.make_async_remote_copy(
            src_ref=partial.at[i, 1 - core],
            dst_ref=from_core.at[i],
            send_sem=core_send.at[i],
            recv_sem=core_recv.at[i],
            device_id=(r, zl * PLANE + y * 2 + 1 - core),
            device_id_type=MESH,
        )

    def sum_cores(i):
        ladder = jnp.transpose(total[i])
        for t in range(PLANE):
            partial[i, t % 2, t // 2] = ladder[8 * t : 8 * t + 8]
        core_copy(i).start()

    def y_copy(i, block, away, target, recv_sem):
        return pltpu.make_async_remote_copy(
            src_ref=partial.at[i, core, (y + 8 + block) % 8],
            dst_ref=target,
            send_sem=y_send.at[i],
            recv_sem=recv_sem,
            device_id=(r, zl * PLANE + (y + 8 + away) % 8 * 2 + core),
            device_id_type=MESH,
        )

    def sum_y(i):
        core_copy(i).wait_recv()
        partial[i, core] = partial[i, core] + from_core[i]
        y_copy(i, 4, 2 - 4 * (i % 2), join.at[i, 2], join_recv.at[i]).start()
        for n, side in enumerate((1, -1)):
            y_copy(i, 3 * side, side, join.at[i, n], join_recv.at[i]).start()
        for n, side in enumerate((1, -1)):
            y_copy(i, side, side, from_y.at[i, n], y_recv.at[i]).start()

    def join_y(i):
        wait_for(join.at[i], join_recv.at[i])
        for n, away in enumerate((2, -2, 2 - 4 * (i % 2))):
            block = (y + 8 + away) % 8
            partial[i, core, block] = partial[i, core, block] + join[i, n]
        for n, side in enumerate((2, -2)):
            y_copy(i, side, side, from_y.at[i, 2 + n], y_recv.at[i]).start()

    def z_copy(i):
        return pltpu.make_async_remote_copy(
            src_ref=to_z.at[i],
            dst_ref=from_z.at[zl],
            send_sem=z_send.at[i],
            recv_sem=z_recv.at[zl],
            device_id=(r, i * PLANE + m),
            device_id_type=MESH,
        )

    def sum_z(i):
        wait_for(from_y.at[i], y_recv.at[i])
        value = partial[i, core, y]
        for j in range(4):
            value = value + from_y[i, j]
        to_z[i] = value

    def give(i):
        @pl.when(zl != i)
        def _():
            z_copy(i).start()

    def drain(i):
        wait_for(units.at[i, pl.ds(0, 14)], unit_send.at[i])
        core_copy(i).wait_send()
        wait_for(partial.at[i, 0, pl.ds(0, 7)], y_send.at[i])

    def pair_step(n, first, s, own):
        @pl.when((n - first - s >= 0) & (n - first - s < 2))
        def _():
            for b in range(2):
                step((n - first - s) * 2 + b, s, own)

    total[...] = jnp.zeros_like(total)
    panel[...] = jnp.zeros_like(panel)
    split_integrals()
    make_units()

    @pl.when(zl < STAGES - 1)
    def _():
        pl.semaphore_wait(half_here, STAGES - 1 - zl)

    to_half()

    @pl.when(zh == 1)
    def _():
        to_facing()

    for i in range(STAGES):
        begin(i)

    def turn(n, carry):
        for s in (4, 3, 2, 1):

            @pl.when(n == s)
            def _(s=s):
                for i in range(STAGES):
                    step(i, s, True)

        for s in (4, 3, 2, 1, 0):
            pair_step(n, OTHER_TURN, s, False)

        @pl.when((n == 1) & (zh == 0))
        def _():
            pl.semaphore_wait(facing_here, STAGES)
            to_facing()

        @pl.when((n == OTHER_TURN + 2) | (n == OTHER_TURN + 3))
        def _():
            for b in range(2):
                add((n - OTHER_TURN - 2) * 2 + b, zh)

        return carry

    lax.fori_loop(1, OTHER_TURN + 4, turn, 0)
    for i in range(STAGES):
        step(i, 4 - i // 2, False)
    for i in (0, 1):
        add(i, 1 - zh)
        sum_cores(i)
    for i in (0, 1):
        sum_y(i)
    for i in (2, 3):
        step(i, 4, False)
        add(i, 1 - zh)
        sum_cores(i)
    for i in (0, 1):
        join_y(i)
    for i in (2, 3):
        sum_y(i)
    for i in (0, 1):
        sum_z(i)
        give(i)
    for i in (2, 3):
        join_y(i)

    for load in loads[2:]:
        load.wait()
    pair = jnp.transpose(
        jnp.concatenate(
            [
                jnp.concatenate([pair_ref[...].astype(F32), jnp.zeros((2, 120), F32)], axis=1),
                jnp.zeros((126, 128), F32),
            ],
            axis=0,
        )
    )[0:8]
    table = lax.broadcasted_iota(jnp.int32, (8, 128), 1).astype(F32)
    occ = occ_ref[...].reshape(1, 128)
    occ_first = jnp.sum(jnp.where(pair[:, 0:1] == table, occ, 0.0), axis=1, keepdims=True)
    occ_second = jnp.sum(jnp.where(pair[:, 1:2] == table, occ, 0.0), axis=1, keepdims=True)
    vir = vir_ref[...].reshape(1, NV)
    blocks = lax.broadcasted_iota(jnp.int32, (1, 8), 1)
    a_pick = jnp.sum(
        jnp.where(blocks == r // 2, aorb_ref[...].astype(F32).reshape(1, 8), 0.0),
        axis=1,
        keepdims=True,
    )
    orbitals = lax.broadcasted_iota(jnp.int32, (1, NV), 1).astype(F32)
    vir_a = jnp.sum(jnp.where(orbitals == a_pick, vir, 0.0), axis=1, keepdims=True)
    vir_b = jnp.where(r % 2 == 0, vir[:, 0:AB], vir[:, AB:NV])
    denom = (occ_first + occ_second) - (vir_a + vir_b)

    wait_for(near_in.at[pl.ds(0, PLANE - 1)], near_send)
    wait_for(far_in.at[pl.ds(0, PLANE - 1)], far_send)
    wait_for(units.at[0, pl.ds(0, 7)], up_send)
    for i in range(STAGES):
        drain(i)
    for i in (2, 3):
        sum_z(i)
        give(i)
    others = other_ref[...]
    for q in range(STAGES - 1):
        source = (zl + 1 + q) % STAGES
        wait_for(from_z.at[source], z_recv.at[source])
        others = others + from_z[source, :, 0:AB]
    out_ref[...] = old_ref[...] + (to_z[zl, :, 0:AB] + others) / denom
    for i in range(STAGES):

        @pl.when(zl != i)
        def _(i=i):
            z_copy(i).wait_send()


def local(
    integrals, amplitudes, old_amps, other_terms, occ_energy, vir_energy, pair_occ, a_orbitals
):
    vmem = pl.BlockSpec(memory_space=pltpu.VMEM)
    dma = pltpu.SemaphoreType.DMA
    return pl.pallas_call(
        kernel,
        out_shape=jax.ShapeDtypeStruct((8, AB), F32),
        in_specs=[pl.BlockSpec(memory_space=pltpu.HBM)] * 8,
        out_specs=vmem,
        scratch_shapes=[
            pltpu.VMEM((AB, NV), F32),
            pltpu.VMEM((8 * 64, DEPTH), F32),
            pltpu.VMEM((8, AB), F32),
            pltpu.VMEM((8, AB), F32),
            pltpu.VMEM((128,), F32),
            pltpu.VMEM((NV,), F32),
            pltpu.VMEM((2, 8), jnp.int32),
            pltpu.VMEM((8,), jnp.int32),
            pltpu.VMEM((PLANE, 8, 128), F32),
            pltpu.VMEM((PLANE, 8, 128), F32),
            pltpu.VMEM((PLANE, 8, 256), F32),
            pltpu.VMEM((PLANE, 8, 256), F32),
            pltpu.VMEM((STAGES - 1, UNIT, 128), F32),
            pltpu.VMEM((STAGES, ROWS, UNIT, 128), F32),
            pltpu.VMEM((ABP, NVP), BF16),
            pltpu.VMEM((ABP, NVP), BF16),
            pltpu.VMEM((2, WINDOW, 128), F32),
            pltpu.VMEM((STAGES, ABP, 128), F32),
            pltpu.VMEM((STAGES, 2, 8, 8, ABP), F32),
            pltpu.VMEM((STAGES, 8, 8, ABP), F32),
            pltpu.VMEM((STAGES, 3, 8, ABP), F32),
            pltpu.VMEM((STAGES, 4, 8, ABP), F32),
            pltpu.VMEM((STAGES, 8, ABP), F32),
            pltpu.VMEM((STAGES, 8, ABP), F32),
            pltpu.SemaphoreType.REGULAR,
            pltpu.SemaphoreType.REGULAR,
            dma((8,)),
            dma,
            dma,
            dma,
            dma,
            dma,
            dma((STAGES,)),
            dma((STAGES,)),
            dma((STAGES, 15)),
            dma((STAGES,)),
            dma((STAGES,)),
            dma((STAGES,)),
            dma((STAGES,)),
            dma((STAGES,)),
            dma((STAGES,)),
            dma((STAGES,)),
        ],
        compiler_params=pltpu.CompilerParams(
            collective_id=0, has_side_effects=True, vmem_limit_bytes=60 * 1024 * 1024
        ),
        cost_estimate=pl.CostEstimate(
            flops=6 * 512 * AB * NV, bytes_accessed=4 * AB * NV, transcendentals=0
        ),
    )(
        integrals,
        amplitudes.reshape(8 * 64, DEPTH),
        old_amps,
        other_terms,
        occ_energy,
        vir_energy,
        pair_occ.T,
        a_orbitals,
    )


def solution(mesh):
    in_specs = (
        P("row", "col"),
        P("col", None, "row"),
        P("col", "row"),
        P("col", "row"),
        P(),
        P(),
        P("col", None),
        P(),
    )
    out_specs = P("col", "row")
    return jax.shard_map(local, mesh=mesh, in_specs=in_specs, out_specs=out_specs, check_vma=False)
```

time: 79.2 us -> 73.9 us (0.933)
  Pallas kernels: 77.1 us -> 71.5 us
    pallas_call x1, Pallas kernels: 77.1 us -> 71.5 us  [local(): pl.pallas_call(kernel, out_shape=jax.ShapeDtypeStruct((8, AB), F32), in_s...]
where the time goes in v3:
time: 73.9 us; the launch traced here: 72.8 us
  Pallas kernels  71.5 us (97%)
  local copies, waits for them, and re-layouts  1.34 us (2%)
    pallas_call x1, Pallas kernels, local(): pl.pallas_call(kernel, out_shape=jax.ShapeDtypeStruct((8, AB), F32), in_s...  71.5 us

profile of v3, /device:TPU:1, one launch (start us, length us, event | category | flops | bytes accessed | tf_op | source)
XLA Modules:
  0.0 72.8 jit_solution(4843095698401407429)
XLA Ops:
  0.0 71.5 %shard_map.82 = f32[8,600]{1,0:T(8,128)} custom-call(f32[600,1200]{1,0:T(8,128)} %integrals_hbm.1, f32[512,75]{1,0:T(8,128)} %bitcast.2, f32[8,600]{1,0:T(8,128)} %old_hbm.1, f32[8,600]{1,0:T(8,128)} %other_hbm.1, f32[128]{0:T(128)} %occ_hbm.1, f32[1200]{0:T(1024)} %vir_hbm.1, s32[2,8]{1,0:T(2,128)} %bitcast.3, s32[8]{0:T(128)} %aorb_hbm.1), custom_call_target="tpu_custom_call" | custom-call | flops 2211840000 | bytes 2880000 | tf_op jit(solution)/shard_map/pallas_call | solution.py:483
  71.5 1.3 %copy.10 = f32[8,600]{1,0:T(8,128)} copy(f32[8,600]{1,0:T(8,128)} %shard_map.82) | data formatting | bytes 38400

commit v4 on v3

--- a/solution.py
+++ b/solution.py
@@ -56,6 +56,7 @@
     high,
     low,
     panel,
+    last_panel,
     total,
     partial,
     from_core,
@@ -230,18 +231,35 @@
     def land(i, lane, h):
         copy_unit(i, lane, h, origin_of(i, lane, h)).wait_recv()
 
+    def multiply(i, start, width, units_here):
+        columns = pl.ds(pl.multiple_of(start, 128), width)
+        hi, lo = split(units_here)
+        both = jnp.dot(
+            high[:, columns], jnp.concatenate([hi, lo], axis=1), preferred_element_type=F32
+        )
+        rest = jnp.dot(low[:, columns], hi, preferred_element_type=F32)
+        total[i] += both[:, 0:128] + (both[:, 128:256] + rest)
+
+    def place(i, plane, u):
+        panel[plane, pl.ds(plane * SHIFT + u * DEPTH, DEPTH), :] = units[i, plane * X + u, 0:DEPTH]
+
     def add(i, plane):
         for u in range(X):
-            panel[plane, pl.ds(plane * SHIFT + u * DEPTH, DEPTH), :] = units[
-                i, plane * X + u, 0:DEPTH
-            ]
-        columns = pl.ds(pl.multiple_of(plane * 512, 128), WINDOW)
-        hi, lo = split(panel[plane])
-        both = jnp.dot(
-            high[:, columns], jnp.concatenate([hi, lo], axis=1), preferred_element_type=F32
-        )
-        rest = jnp.dot(low[:, columns], hi, preferred_element_type=F32)
-        total[i] += both[:, 0:128] + (both[:, 128:256] + rest)
+            place(i, plane, u)
+        multiply(i, plane * 512, WINDOW, panel[plane])
+
+    other, farthest = 1 - zh, (x + X // 2) % X
+    last_row = other * SHIFT + farthest * DEPTH
+
+    def add_first(i):
+        for n in range(1, X):
+            place(i, other, (farthest + n) % X)
+        panel[other, pl.ds(last_row, DEPTH), :] = jnp.zeros((DEPTH, 128), F32)
+        multiply(i, other * 512, WINDOW, panel[other])
+
+    def add_last(i):
+        last_panel[pl.ds(last_row % 128, DEPTH), :] = units[i, other * X + farthest, 0:DEPTH]
+        multiply(i, other * 512 + last_row // 128 * 128, 256, last_panel[...])
 
     def unit_to(source, plane, row, recv_sem):
         return pltpu.make_async_remote_copy(
@@ -366,6 +384,7 @@
 
     total[...] = jnp.zeros_like(total)
     panel[...] = jnp.zeros_like(panel)
+    last_panel[...] = jnp.zeros_like(last_panel)
     split_integrals()
     make_units()
 
@@ -403,19 +422,26 @@
             for b in range(2):
                 add((n - OTHER_TURN - 2) * 2 + b, zh)
 
+        @pl.when(n == OTHER_TURN + 3)
+        def _():
+            add_first(0)
+            add_first(1)
+
         return carry
 
     lax.fori_loop(1, OTHER_TURN + 4, turn, 0)
     for i in range(STAGES):
         step(i, 4 - i // 2, False)
     for i in (0, 1):
-        add(i, 1 - zh)
+        add_last(i)
         sum_cores(i)
+    for i in (2, 3):
+        add_first(i)
     for i in (0, 1):
         sum_y(i)
     for i in (2, 3):
         step(i, 4, False)
-        add(i, 1 - zh)
+        add_last(i)
         sum_cores(i)
     for i in (0, 1):
         join_y(i)
@@ -503,6 +529,7 @@
             pltpu.VMEM((ABP, NVP), BF16),
             pltpu.VMEM((ABP, NVP), BF16),
             pltpu.VMEM((2, WINDOW, 128), F32),
+            pltpu.VMEM((256, 128), F32),
             pltpu.VMEM((STAGES, ABP, 128), F32),
             pltpu.VMEM((STAGES, 2, 8, 8, ABP), F32),
             pltpu.VMEM((STAGES, 8, 8, ABP), F32),

time: 73.9 us -> 73.1 us (0.989)
  the two profiles are of different devices: /device:TPU:1 before, /device:TPU:16 now
where the time goes in v4:
time: 73.1 us; the launch traced here: 72.9 us
  Pallas kernels  71.5 us (98%)
  local copies, waits for them, and re-layouts  1.34 us (2%)
    pallas_call x1, Pallas kernels, local(): pl.pallas_call(kernel, out_shape=jax.ShapeDtypeStruct((8, AB), F32), in_s...  71.5 us

profile of v4, /device:TPU:16, one launch (start us, length us, event | category | flops | bytes accessed | tf_op | source)
XLA Modules:
  0.0 72.9 jit_solution(7425544264457767433)
XLA Ops:
  0.0 71.5 %shard_map.82 = f32[8,600]{1,0:T(8,128)} custom-call(f32[600,1200]{1,0:T(8,128)} %integrals_hbm.1, f32[512,75]{1,0:T(8,128)} %bitcast.2, f32[8,600]{1,0:T(8,128)} %old_hbm.1, f32[8,600]{1,0:T(8,128)} %other_hbm.1, f32[128]{0:T(128)} %occ_hbm.1, f32[1200]{0:T(1024)} %vir_hbm.1, s32[2,8]{1,0:T(2,128)} %bitcast.3, s32[8]{0:T(128)} %aorb_hbm.1), custom_call_target="tpu_custom_call" | custom-call | flops 2211840000 | bytes 2880000 | tf_op jit(solution)/shard_map/pallas_call | solution.py:509
  71.5 1.3 %copy.10 = f32[8,600]{1,0:T(8,128)} copy(f32[8,600]{1,0:T(8,128)} %shard_map.82) | data formatting | bytes 38400

commit v5 on v4

--- a/solution.py
+++ b/solution.py
@@ -388,15 +388,15 @@
     split_integrals()
     make_units()
 
+    @pl.when(zh == 1)
+    def _():
+        to_facing()
+
     @pl.when(zl < STAGES - 1)
     def _():
         pl.semaphore_wait(half_here, STAGES - 1 - zl)
 
     to_half()
-
-    @pl.when(zh == 1)
-    def _():
-        to_facing()
 
     for i in range(STAGES):
         begin(i)

time: 73.1 us -> 74.1 us (1.014)
  the two profiles are of different devices: /device:TPU:16 before, /device:TPU:512 now
where the time goes in v5:
time: 74.1 us; the launch traced here: 73.8 us
  Pallas kernels  72.5 us (98%)
  local copies, waits for them, and re-layouts  1.34 us (2%)
    pallas_call x1, Pallas kernels, local(): pl.pallas_call(kernel, out_shape=jax.ShapeDtypeStruct((8, AB), F32), in_s...  72.5 us

profile of v5, /device:TPU:512, one launch (start us, length us, event | category | flops | bytes accessed | tf_op | source)
XLA Modules:
  0.0 73.8 jit_solution(12092840661466947040)
XLA Ops:
  0.0 72.5 %shard_map.82 = f32[8,600]{1,0:T(8,128)} custom-call(f32[600,1200]{1,0:T(8,128)} %integrals_hbm.1, f32[512,75]{1,0:T(8,128)} %bitcast.2, f32[8,600]{1,0:T(8,128)} %old_hbm.1, f32[8,600]{1,0:T(8,128)} %other_hbm.1, f32[128]{0:T(128)} %occ_hbm.1, f32[1200]{0:T(1024)} %vir_hbm.1, s32[2,8]{1,0:T(2,128)} %bitcast.3, s32[8]{0:T(128)} %aorb_hbm.1), custom_call_target="tpu_custom_call" | custom-call | flops 2211840000 | bytes 2880000 | tf_op jit(solution)/shard_map/pallas_call | solution.py:509
  72.5 1.3 %copy.10 = f32[8,600]{1,0:T(8,128)} copy(f32[8,600]{1,0:T(8,128)} %shard_map.82) | data formatting | bytes 38400
